TPU v7x, 512 devices: a whole 4x4x16 slice. The times are simulated.
512 devices in a mesh: grp: 16 (over x, y), dev: 32 (over z, core).
Axes of the slice: x: 4, y: 4, z: 16, core: 2. Of those that a mesh axis runs over, the one named last changes fastest.
Arguments:
- block_vectors: float32 [262144, 64], P(('grp', 'dev')), may hold values from -6 to 6
- hamiltonian: float32 [4096, 64, 2048], P(('grp', 'dev')), may hold values from -0.125 to 0.125
- pattern: int32 [4096, 32], P(('grp', 'dev')), may hold values from 0 to 4095, as said below
- owned_blocks: int32 [512], P(('grp', 'dev')), may hold values from 1 to 8, as said below
- spectrum: float32 [2], replicated, may hold values from 0.5 to 2
Outputs:
- basis: float32 [262144, 64], P(('grp', 'dev'))
- r_factor: float32 [64, 64], replicated
Inputs may be any that keep to these rules, and one draw needn't show every extreme that they name: pattern[b, 0] = b; every other entry is b + o clipped to the slots, for a distinct nonzero o with |o| <= 16. `owned_blocks`: some device owns all 8 slots.
All inputs are finite; a program needn't handle non-finite values.
Results may differ from a plain program's by a relative error of at most 0.0003.
Values sent between devices are 32-bit elements; how exact they have to be, the bound alone decides.
A program may use at most 64 MiB of HBM per device.

v0:
```python
import jax
import jax.numpy as jnp
from jax import lax
from jax.sharding import PartitionSpec as P

BAND = 16


def shifted(block, axis, distance):
    devices = range(lax.axis_size(axis))
    route = [(i - distance, i) for i in devices if i - distance in devices]
    return lax.ppermute(block, axis, route)


def send_direct(values, distance):
    return shifted(values, ("grp", "dev"), distance)


def extend_band(values, reach_dev):
    lowers = []
    uppers = []
    for distance in range(reach_dev, 0, -1):
        lowers.append(send_direct(values, distance))
    for distance in range(1, reach_dev + 1):
        uppers.append(send_direct(values, -distance))
    return jnp.concatenate(lowers + [values] + uppers, axis=0)


def apply_matrix(values, hamiltonian, local_index, reach_dev):
    extended = extend_band(values, reach_dev)
    block_count, neighbours = local_index.shape
    picked = jnp.take(extended, local_index, axis=0)
    picked = picked.reshape(block_count, neighbours * values.shape[1], values.shape[2])
    return jnp.einsum("gik,gkc->gic", hamiltonian, picked, precision=lax.Precision.HIGHEST)


def summed_gram(flat):
    local_gram = jnp.dot(
        flat.T, flat, precision=lax.Precision.HIGHEST, preferred_element_type=jnp.float32
    )
    return lax.psum(local_gram, ("grp", "dev"))


def cholesky_step(flat):
    gram_total = summed_gram(flat)
    upper = jnp.linalg.cholesky(gram_total).T
    ortho = jax.scipy.linalg.solve_triangular(upper.T, flat.T, lower=True).T
    return (ortho, upper)


def on_device(block_vectors, hamiltonian, pattern, owned_blocks, spectrum):
    block_count = pattern.shape[0]
    block_size = hamiltonian.shape[1]
    columns = block_vectors.shape[1]
    reach_dev = (BAND + block_count - 1) // block_count
    first_block = lax.axis_index(("grp", "dev")) * block_count
    local_index = pattern - first_block + reach_dev * block_count
    live_mask = (jnp.arange(block_count, dtype=jnp.int32) < owned_blocks[0]).astype(jnp.float32)[
        :, None, None
    ]
    shift_value = spectrum[0]
    scale_value = spectrum[1]
    first_vec = block_vectors.reshape(block_count, block_size, columns) * live_mask
    second_vec = live_mask * (
        (apply_matrix(first_vec, hamiltonian, local_index, reach_dev) - shift_value * first_vec)
        / scale_value
    )
    third_vec = live_mask * (
        2.0
        * (apply_matrix(second_vec, hamiltonian, local_index, reach_dev) - shift_value * second_vec)
        / scale_value
        - first_vec
    )
    flat = third_vec.reshape(block_count * block_size, columns)
    ortho_one, upper_one = cholesky_step(flat)
    ortho_two, upper_two = cholesky_step(ortho_one)
    upper_all = jnp.dot(
        upper_two, upper_one, precision=lax.Precision.HIGHEST, preferred_element_type=jnp.float32
    )
    total = jnp.sqrt(
        jnp.float32(block_count * block_size * lax.axis_size("grp") * lax.axis_size("dev"))
    )
    return (ortho_two * total, upper_all / total)


def solution(mesh):
    placed = (
        P(("grp", "dev"), None),
        P(("grp", "dev"), None, None),
        P(("grp", "dev"), None),
        P(("grp", "dev")),
        P(),
    )
    return jax.shard_map(
        on_device,
        mesh=mesh,
        in_specs=placed,
        out_specs=(P(("grp", "dev"), None), P()),
        check_vma=False,
    )
```

profile of v0, /device:TPU:1, one launch (start us, length us, event | category | flops | bytes accessed | tf_op | source)
XLA Modules:
  0.0 355.4 jit_solution(15956783039810358615)
XLA Ops:
  3.7 8.8 %collective-permute-start.2 = (f32[8,64,64]{1,2,0:T(8,128)S(1)}, f32[8,64,64]{1,2,0:T(8,128)S(1)}, u32[]{:S(2)}, u32[]{:S(2)}) collective-permute-start(f32[8,64,64]{1,2,0:T(8,128)S(1)} %copy_multiply_fusion), channel_id=1, source_target_pairs={{1,0},{2,1},{3,2},{4,3},{5,4},{6,5},{7,6},{8,7},{9,8},{10,9},{11,1... | collective-permute-start | bytes 393224 | tf_op jit(solution)/shard_map/ppermute | solution.py:12
  12.5 4.2 %collective-permute-start.1 = (f32[8,64,64]{1,2,0:T(8,128)S(1)}, f32[8,64,64]{1,2,0:T(8,128)S(1)}, u32[]{:S(2)}, u32[]{:S(2)}) collective-permute-start(f32[8,64,64]{1,2,0:T(8,128)S(1)} %copy_multiply_fusion), channel_id=1, source_target_pairs={{0,1},{1,2},{2,3},{3,4},{4,5},{5,6},{6,7},{7,8},{8,9},{9,10},{10,1... | collective-permute-start | bytes 393224 | tf_op jit(solution)/shard_map/ppermute | solution.py:12
  20.8 4.5 %collective-permute-done = f32[8,64,64]{1,2,0:T(8,128)S(1)} collective-permute-done((f32[8,64,64]{1,2,0:T(8,128)S(1)}, f32[8,64,64]{1,2,0:T(8,128)S(1)}, u32[]{:S(2)}, u32[]{:S(2)}) %collective-permute-start) | collective-permute-done | bytes 131104 | tf_op jit(solution)/shard_map/ppermute | solution.py:12
  25.6 4.4 %gather_fusion = f32[256,64,64]{1,2,0:T(8,128)} fusion(f32[40,64,64]{1,2,0:T(8,128)S(1)} %constant_dynamic-update-slice_fusion, s32[1024]{0:T(1024)S(1)} %pad_clamp_fusion), kind=kCustom, calls=%fused_computation.clone | custom fusion | bytes 8389632 | tf_op jit(solution)/shard_map/jit(_take)/gather | solution.py:32
  29.9 3.8 %broadcast_select_fusion.1 = f32[8,32,64,64]{2,3,1,0:T(8,128)S(1)} fusion(f32[8,32,64,64]{2,3,1,0:T(8,128)} %bitcast.73, pred[8,32]{1,0:T(8,128)(4,1)S(1)} %get-tuple-element.4), kind=kLoop, calls=%fused_computation.3 | loop fusion | flops 1048576 | bytes 8388864 | tf_op jit(solution)/shard_map/jit(_take)/select_n | solution.py:32
  33.8 8.0 %copy.15 = f32[8,32,64,64]{2,1,3,0:T(8,128)} copy(f32[8,32,64,64]{2,3,1,0:T(8,128)S(1)} %broadcast_select_fusion.1) | data formatting | bytes 8388608 | tf_op jit(solution)/shard_map/jit(_take)/select_n | solution.py:32
  41.8 7.8 %reshape.35 = f32[8,2048,64]{1,2,0:T(8,128)} reshape(f32[8,32,64,64]{2,1,3,0:T(8,128)} %copy.15) | data formatting | bytes 8388608 | tf_op jit(solution)/shard_map/reshape | solution.py:33
  49.6 8.7 %fusion.4 = f32[8,64,64]{1,2,0:T(8,128)S(1)} fusion(f32[8,2048,64]{1,2,0:T(8,128)} %reshape.35, f32[8,64,2048]{2,1,0:T(8,128)} %param.11, f32[]{:T(128)} %bitcast.4, f32[]{:T(128)} %bitcast.3, f32[8]{0:T(128)S(1)} %compare_convert_fusion, f32[8,64,64]{1,0,2:T(8,128)S(1)} %reshape.34), kind=kOutput, calls=%fused_computation.10 | convolution fusion | flops 805470208 | bytes 8650792 | tf_op jit(solution)/shard_map/gik,gkc->gic/dot_general | solution.py:34
  58.3 4.1 %collective-permute-start.4 = (f32[8,64,64]{1,2,0:T(8,128)S(1)}, f32[8,64,64]{1,2,0:T(8,128)S(1)}, u32[]{:S(2)}, u32[]{:S(2)}) collective-permute-start(f32[8,64,64]{1,2,0:T(8,128)S(1)} %fusion.4), channel_id=1, source_target_pairs={{0,2},{1,3},{2,4},{3,5},{4,6},{5,7},{6,8},{7,9},{8,10},{9,11},{10,... | collective-permute-start | bytes 393224 | tf_op jit(solution)/shard_map/ppermute | solution.py:12
  62.4 2.7 collective-permute-start.5
  68.5 2.8 collective-permute-done.5
  71.3 6.5 %collective-permute-done.6 = f32[8,64,64]{1,2,0:T(8,128)S(1)} collective-permute-done((f32[8,64,64]{1,2,0:T(8,128)S(1)}, f32[8,64,64]{1,2,0:T(8,128)S(1)}, u32[]{:S(2)}, u32[]{:S(2)}) %collective-permute-start.6) | collective-permute-done | bytes 131104 | tf_op jit(solution)/shard_map/ppermute | solution.py:12
  77.9 4.4 %gather_fusion.1 = f32[256,64,64]{1,2,0:T(8,128)} fusion(f32[40,64,64]{1,2,0:T(8,128)S(1)} %constant_dynamic-update-slice_fusion.5, s32[1024]{0:T(1024)S(1)} %pad_clamp_fusion), kind=kCustom, calls=%fused_computation.1.clone | custom fusion | bytes 8389632 | tf_op jit(solution)/shard_map/jit(_take)/gather | solution.py:32
  82.2 3.8 %broadcast_select_fusion = f32[8,32,64,64]{2,3,1,0:T(8,128)S(1)} fusion(f32[8,32,64,64]{2,3,1,0:T(8,128)} %bitcast.72, pred[8,32]{1,0:T(8,128)(4,1)S(1)} %get-tuple-element.4), kind=kLoop, calls=%fused_computation.2 | loop fusion | flops 1048576 | bytes 8388864 | tf_op jit(solution)/shard_map/jit(_take)/select_n | solution.py:32
  86.1 8.0 %copy.16 = f32[8,32,64,64]{2,1,3,0:T(8,128)} copy(f32[8,32,64,64]{2,3,1,0:T(8,128)S(1)} %broadcast_select_fusion) | data formatting | bytes 8388608 | tf_op jit(solution)/shard_map/jit(_take)/select_n | solution.py:32
  94.1 7.8 %reshape.36 = f32[8,2048,64]{1,2,0:T(8,128)} reshape(f32[8,32,64,64]{2,1,3,0:T(8,128)} %copy.16) | data formatting | bytes 8388608 | tf_op jit(solution)/shard_map/reshape | solution.py:33
  101.9 8.7 %fusion.7 = f32[8,64,64]{1,2,0:T(8,128)S(1)} fusion(f32[8,2048,64]{1,2,0:T(8,128)} %reshape.36, f32[8,64,2048]{2,1,0:T(8,128)} %param.11, f32[8,64,64]{1,2,0:T(8,128)S(1)} %fusion.4, f32[]{:T(128)} %bitcast.4, f32[]{:T(128)} %bitcast.3, f32[8]{0:T(128)S(1)} %compare_convert_fusion, f32[8,64,64]{1,0,2:T(8,128)S(1)} %reshape.34), kind=kOutput, calls=%fused_computation.13 | convolution fusion | flops 805535744 | bytes 8781864 | tf_op jit(solution)/shard_map/gik,gkc->gic/dot_general | solution.py:34
  111.1 116.5 %psum.14 = f32[64,64]{0,1:T(8,128)S(1)} all-reduce(f32[64,64]{0,1:T(8,128)S(1)} %convolution_bitcast_fusion.2), channel_id=1, replica_groups=mesh['grp'=16,'dev'=32] {'grp','dev'}, use_global_device_ids=true, to_apply=%region_0.0 | all-reduce | flops 4096 | bytes 32768 | tf_op jit(solution)/shard_map/psum | solution.py:41
  227.9 5.8 %cholesky.44 = f32[64,64]{1,0:T(8,128)S(1)} custom-call(f32[64,64]{1,0:T(8,128)S(1)} %fusion.14), custom_call_target="Cholesky" | custom-call | tf_op jit(solution)/shard_map/jit(cholesky)/cholesky | solution.py:46
  235.1 4.9 %custom-call.6 = f32[1,64,64]{1,2,0:T(8,128)S(1)} custom-call(f32[1,64,64]{2,1,0:T(8,128)S(1)} %fusion.18), custom_call_target="InvertDiagBlocksLowerTriangular" | custom-call | tf_op jit(solution)/shard_map/jit(_solve_triangular)/triangular_solve | solution.py:47
  240.6 99.3 %psum.15 = f32[64,64]{0,1:T(8,128)S(1)} all-reduce(f32[64,64]{0,1:T(8,128)S(1)} %fusion.30), channel_id=1, replica_groups=mesh['grp'=16,'dev'=32] {'grp','dev'}, use_global_device_ids=true, to_apply=%region_3.7 | all-reduce | flops 4096 | bytes 32768 | tf_op jit(solution)/shard_map/psum | solution.py:41
  340.0 5.8 %cholesky.55 = f32[64,64]{1,0:T(8,128)S(1)} custom-call(f32[64,64]{1,0:T(8,128)S(1)} %fusion.12), custom_call_target="Cholesky" | custom-call | tf_op jit(solution)/shard_map/jit(cholesky)/cholesky | solution.py:46
  346.6 2.2 convolution_multiply_fusion.1
  349.5 4.9 %custom-call.7 = f32[1,64,64]{1,2,0:T(8,128)S(1)} custom-call(f32[1,64,64]{2,1,0:T(8,128)S(1)} %select_bitcast_fusion), custom_call_target="InvertDiagBlocksLowerTriangular" | custom-call | tf_op jit(solution)/shard_map/jit(_solve_triangular)/triangular_solve | solution.py:47
  (42 shorter events, 15.4 us)
Async XLA Ops:
  2.4 23.1 %collective-permute-start.3 = (f32[8,64,64]{1,2,0:T(8,128)S(1)}, f32[8,64,64]{1,2,0:T(8,128)S(1)}, u32[]{:S(2)}, u32[]{:S(2)}) collective-permute-start(f32[8,64,64]{1,2,0:T(8,128)S(1)} %copy_multiply_fusion), channel_id=1, source_target_pairs={{2,0},{3,1},{4,2},{5,3},{6,4},{7,5},{8,6},{9,7},{10,8},{11,9},{12,... | collective-permute-start | bytes 393224 | tf_op jit(solution)/shard_map/ppermute | solution.py:12
  3.7 21.8 %collective-permute-start.2 = (f32[8,64,64]{1,2,0:T(8,128)S(1)}, f32[8,64,64]{1,2,0:T(8,128)S(1)}, u32[]{:S(2)}, u32[]{:S(2)}) collective-permute-start(f32[8,64,64]{1,2,0:T(8,128)S(1)} %copy_multiply_fusion), channel_id=1, source_target_pairs={{1,0},{2,1},{3,2},{4,3},{5,4},{6,5},{7,6},{8,7},{9,8},{10,9},{11,1... | collective-permute-start | bytes 393224 | tf_op jit(solution)/shard_map/ppermute | solution.py:12
  12.5 12.9 %collective-permute-start.1 = (f32[8,64,64]{1,2,0:T(8,128)S(1)}, f32[8,64,64]{1,2,0:T(8,128)S(1)}, u32[]{:S(2)}, u32[]{:S(2)}) collective-permute-start(f32[8,64,64]{1,2,0:T(8,128)S(1)} %copy_multiply_fusion), channel_id=1, source_target_pairs={{0,1},{1,2},{2,3},{3,4},{4,5},{5,6},{6,7},{7,8},{8,9},{9,10},{10,1... | collective-permute-start | bytes 393224 | tf_op jit(solution)/shard_map/ppermute | solution.py:12
  16.7 8.7 %collective-permute-start = (f32[8,64,64]{1,2,0:T(8,128)S(1)}, f32[8,64,64]{1,2,0:T(8,128)S(1)}, u32[]{:S(2)}, u32[]{:S(2)}) collective-permute-start(f32[8,64,64]{1,2,0:T(8,128)S(1)} %copy_multiply_fusion), channel_id=1, source_target_pairs={{0,2},{1,3},{2,4},{3,5},{4,6},{5,7},{6,8},{7,9},{8,10},{9,11},{10,... | collective-permute-start | bytes 393224 | tf_op jit(solution)/shard_map/ppermute | solution.py:12
  58.3 10.2 %collective-permute-start.4 = (f32[8,64,64]{1,2,0:T(8,128)S(1)}, f32[8,64,64]{1,2,0:T(8,128)S(1)}, u32[]{:S(2)}, u32[]{:S(2)}) collective-permute-start(f32[8,64,64]{1,2,0:T(8,128)S(1)} %fusion.4), channel_id=1, source_target_pairs={{0,2},{1,3},{2,4},{3,5},{4,6},{5,7},{6,8},{7,9},{8,10},{9,11},{10,... | collective-permute-start | bytes 393224 | tf_op jit(solution)/shard_map/ppermute | solution.py:12
  62.4 8.9 %collective-permute-start.5 = (f32[8,64,64]{1,2,0:T(8,128)S(1)}, f32[8,64,64]{1,2,0:T(8,128)S(1)}, u32[]{:S(2)}, u32[]{:S(2)}) collective-permute-start(f32[8,64,64]{1,2,0:T(8,128)S(1)} %fusion.4), channel_id=1, source_target_pairs={{0,1},{1,2},{2,3},{3,4},{4,5},{5,6},{6,7},{7,8},{8,9},{9,10},{10,1... | collective-permute-start | bytes 393224 | tf_op jit(solution)/shard_map/ppermute | solution.py:12
  65.1 12.8 %collective-permute-start.7 = (f32[8,64,64]{1,2,0:T(8,128)S(1)}, f32[8,64,64]{1,2,0:T(8,128)S(1)}, u32[]{:S(2)}, u32[]{:S(2)}) collective-permute-start(f32[8,64,64]{1,2,0:T(8,128)S(1)} %fusion.4), channel_id=1, source_target_pairs={{2,0},{3,1},{4,2},{5,3},{6,4},{7,5},{8,6},{9,7},{10,8},{11,9},{12,... | collective-permute-start | bytes 393224 | tf_op jit(solution)/shard_map/ppermute | solution.py:12
  66.4 11.4 %collective-permute-start.6 = (f32[8,64,64]{1,2,0:T(8,128)S(1)}, f32[8,64,64]{1,2,0:T(8,128)S(1)}, u32[]{:S(2)}, u32[]{:S(2)}) collective-permute-start(f32[8,64,64]{1,2,0:T(8,128)S(1)} %fusion.4), channel_id=1, source_target_pairs={{1,0},{2,1},{3,2},{4,3},{5,4},{6,5},{7,6},{8,7},{9,8},{10,9},{11,1... | collective-permute-start | bytes 393224 | tf_op jit(solution)/shard_map/ppermute | solution.py:12
where the time goes:
time: 356 us; the launch traced here: 355 us
  blocking collectives  216 us (61%)
  local copies, waits for them, and re-layouts  43.3 us (12%)
  other arithmetic  32.9 us (9%)
  starting transfers between devices  26.5 us (7%)
  matrix products  21.5 us (6%)
  waiting for transfers between devices  13.8 us (4%)
    psum x2, blocking collectives, summed_gram(): return lax.psum(local_gram, ('grp', 'dev'))  216 us
    ppermute x8, starting transfers between devices, shifted(): return lax.ppermute(block, axis, route)  26.5 us
    dot_general x2, matrix products, apply_matrix(): jnp.einsum('gik,gkc->gic', hamiltonian, picked, precision=lax.Precision.H...  17.4 us
    select_n x2, local copies, waits for them, and re-layouts, apply_matrix(): picked = jnp.take(extended, local_index, axis=0)  16 us
    reshape x2, local copies, waits for them, and re-layouts, apply_matrix(): picked.reshape(block_count, neighbours * values.shape[1], values.shape[2])  15.6 us
    ppermute x8, waiting for transfers between devices, shifted(): return lax.ppermute(block, axis, route)  13.8 us
    another operation x6, other arithmetic, cholesky_step(): upper = jnp.linalg.cholesky(gram_total).T  13.1 us
    another operation x4, other arithmetic, cholesky_step(): ortho = jax.scipy.linalg.solve_triangular(upper.T, flat.T, lower=True).T  11.1 us
  transfers between devices with their start and end apart: 8, of which 3 were waited for; matrix products, arithmetic and copies ran while one was open for 1% of the time, Pallas kernels for 0%

commit v1 on v0

--- a/solution.py
+++ b/solution.py
@@ -38,7 +38,7 @@
     local_gram = jnp.dot(
         flat.T, flat, precision=lax.Precision.HIGHEST, preferred_element_type=jnp.float32
     )
-    return lax.psum(local_gram, ("grp", "dev"))
+    return jnp.sum(lax.all_gather(local_gram, ("grp", "dev")), axis=0)
 
 
 def cholesky_step(flat):

time: 356 us -> 611 us (1.72)
  waiting for transfers between devices: 13.8 us -> 456 us
  blocking collectives: 216 us -> 0 us
  other arithmetic: 32.9 us -> 46.7 us
  between operations: 1.58 us -> 15 us
    all_gather x0 -> x2, waiting for transfers between devices: none -> 442 us  [summed_gram(): return jnp.sum(lax.all_gather(local_gram, ('grp', 'dev')), axis=0)]
    psum x2 -> x0, blocking collectives: 216 us -> none  [summed_gram(): return lax.psum(local_gram, ('grp', 'dev'))]
    reduce_sum x0 -> x2, other arithmetic: none -> 13.9 us  [summed_gram(): return jnp.sum(lax.all_gather(local_gram, ('grp', 'dev')), axis=0)]
  transfers between devices with their start and end apart: 8 -> 10, of which waited for: 3 -> 5; matrix products, arithmetic and copies ran while one was open for 1% -> 0% of each run, Pallas kernels for 0% -> 0%
where the time goes in v1:
time: 611 us
  waiting for transfers between devices  456 us (75%)
  other arithmetic  46.7 us (8%)
  local copies, waits for them, and re-layouts  43.3 us (7%)
  starting transfers between devices  26.8 us (4%)
  matrix products  22.7 us (4%)
  between operations  15 us (2%)
    all_gather x2, waiting for transfers between devices, summed_gram(): return jnp.sum(lax.all_gather(local_gram, ('grp', 'dev')), axis=0)  442 us
    ppermute x8, starting transfers between devices, shifted(): return lax.ppermute(block, axis, route)  26.5 us
    dot_general x2, matrix products, apply_matrix(): jnp.einsum('gik,gkc->gic', hamiltonian, picked, precision=lax.Precision.H...  17.4 us
    select_n x2, local copies, waits for them, and re-layouts, apply_matrix(): picked = jnp.take(extended, local_index, axis=0)  16 us
    reshape x2, local copies, waits for them, and re-layouts, apply_matrix(): picked.reshape(block_count, neighbours * values.shape[1], values.shape[2])  15.6 us
    ppermute x8, waiting for transfers between devices, shifted(): return lax.ppermute(block, axis, route)  14 us
    reduce_sum x2, other arithmetic, summed_gram(): return jnp.sum(lax.all_gather(local_gram, ('grp', 'dev')), axis=0)  13.9 us
    another operation x6, other arithmetic, cholesky_step(): upper = jnp.linalg.cholesky(gram_total).T  13.1 us
  transfers between devices with their start and end apart: 10, of which 5 were waited for; matrix products, arithmetic and copies ran while one was open for 0% of the time, Pallas kernels for 0%

profile of v1, /device:TPU:1, one launch (start us, length us, event | category | flops | bytes accessed | tf_op | source)
XLA Modules:
  0.0 610.5 jit_solution(17217625274676176439)
XLA Ops:
  10.3 8.8 %collective-permute-start.2 = (f32[8,64,64]{1,2,0:T(8,128)S(1)}, f32[8,64,64]{1,2,0:T(8,128)S(1)}, u32[]{:S(2)}, u32[]{:S(2)}) collective-permute-start(f32[8,64,64]{1,2,0:T(8,128)S(1)} %copy_multiply_fusion), channel_id=1, source_target_pairs={{1,0},{2,1},{3,2},{4,3},{5,4},{6,5},{7,6},{8,7},{9,8},{10,9},{11,1... | collective-permute-start | bytes 393224 | tf_op jit(solution)/shard_map/ppermute | solution.py:12
  19.1 4.2 collective-permute-start.1
  27.4 4.5 collective-permute-done
  32.1 4.4 gather_fusion
  36.5 3.8 broadcast_select_fusion.1
  40.3 8.0 %copy.20 = f32[8,32,64,64]{2,1,3,0:T(8,128)} copy(f32[8,32,64,64]{2,3,1,0:T(8,128)S(1)} %broadcast_select_fusion.1) | data formatting | bytes 8388608 | tf_op jit(solution)/shard_map/jit(_take)/select_n | solution.py:32
  48.3 7.8 %reshape.35 = f32[8,2048,64]{1,2,0:T(8,128)} reshape(f32[8,32,64,64]{2,1,3,0:T(8,128)} %copy.20) | data formatting | bytes 8388608 | tf_op jit(solution)/shard_map/reshape | solution.py:33
  56.2 8.7 %fusion.4 = f32[8,64,64]{1,2,0:T(8,128)S(1)} fusion(f32[8,2048,64]{1,2,0:T(8,128)} %reshape.35, f32[8,64,2048]{2,1,0:T(8,128)} %param.11, f32[]{:T(128)} %bitcast.4, f32[]{:T(128)} %bitcast.3, f32[8]{0:T(128)S(1)} %compare_convert_fusion, f32[8,64,64]{1,0,2:T(8,128)S(1)} %reshape.34), kind=kOutput, calls=%fused_computation.10 | convolution fusion | flops 805470208 | bytes 8650792 | tf_op jit(solution)/shard_map/gik,gkc->gic/dot_general | solution.py:34
  64.8 4.1 collective-permute-start.4
  75.1 2.8 collective-permute-done.5
  77.9 6.7 %collective-permute-done.6 = f32[8,64,64]{1,2,0:T(8,128)S(1)} collective-permute-done((f32[8,64,64]{1,2,0:T(8,128)S(1)}, f32[8,64,64]{1,2,0:T(8,128)S(1)}, u32[]{:S(2)}, u32[]{:S(2)}) %collective-permute-start.6) | collective-permute-done | bytes 131104 | tf_op jit(solution)/shard_map/ppermute | solution.py:12
  84.6 4.4 gather_fusion.1
  89.0 3.8 broadcast_select_fusion
  92.8 8.0 %copy.21 = f32[8,32,64,64]{2,1,3,0:T(8,128)} copy(f32[8,32,64,64]{2,3,1,0:T(8,128)S(1)} %broadcast_select_fusion) | data formatting | bytes 8388608 | tf_op jit(solution)/shard_map/jit(_take)/select_n | solution.py:32
  100.8 7.8 %reshape.36 = f32[8,2048,64]{1,2,0:T(8,128)} reshape(f32[8,32,64,64]{2,1,3,0:T(8,128)} %copy.21) | data formatting | bytes 8388608 | tf_op jit(solution)/shard_map/reshape | solution.py:33
  108.7 8.7 %fusion.7 = f32[8,64,64]{1,2,0:T(8,128)S(1)} fusion(f32[8,2048,64]{1,2,0:T(8,128)} %reshape.36, f32[8,64,2048]{2,1,0:T(8,128)} %param.11, f32[8,64,64]{1,2,0:T(8,128)S(1)} %fusion.4, f32[]{:T(128)} %bitcast.4, f32[]{:T(128)} %bitcast.3, f32[8]{0:T(128)S(1)} %compare_convert_fusion, f32[8,64,64]{1,0,2:T(8,128)S(1)} %reshape.34), kind=kOutput, calls=%fused_computation.13 | convolution fusion | flops 805535744 | bytes 8781864 | tf_op jit(solution)/shard_map/gik,gkc->gic/dot_general | solution.py:34
  118.9 226.5 %all-gather.5.cloned.1.call-done = f32[32768,64]{1,0:T(8,128)} async-done(((f32[64,64]{1,0:T(8,128)}), f32[32768,64]{1,0:T(8,128)}) %all-gather.5.cloned.1.call-update) | async-done | bytes 8388624 | tf_op jit(solution)/shard_map/all_gather | solution.py:41
  345.4 6.9 %reduce_sum.18 = f32[64,64]{1,0:T(8,128)S(1)} reduce(f32[512,64,64]{2,1,0:T(8,128)} %bitcast.76, f32[]{:T(128)} %constant.62.clone.1), dimensions={0}, to_apply=%region_0.0 | reduce | flops 2093056 | bytes 8404996 | tf_op jit(solution)/shard_map/reduce_sum | solution.py:41
  352.4 5.8 cholesky.44
  359.6 4.9 custom-call.6
  365.7 215.5 %all-gather.7.cloned.1.call-done = f32[32768,64]{1,0:T(8,128)} async-done(((f32[64,64]{1,0:T(8,128)}), f32[32768,64]{1,0:T(8,128)}) %all-gather.7.cloned.1.call-update) | async-done | bytes 8388624 | tf_op jit(solution)/shard_map/all_gather | solution.py:41
  581.2 6.9 %reduce_sum.19 = f32[64,64]{1,0:T(8,128)S(1)} reduce(f32[512,64,64]{2,1,0:T(8,128)} %bitcast.77, f32[]{:T(128)} %constant.62.clone.1), dimensions={0}, to_apply=%region_3.7 | reduce | flops 2093056 | bytes 8404996 | tf_op jit(solution)/shard_map/reduce_sum | solution.py:41
  588.3 5.8 cholesky.55
  597.8 4.9 custom-call.7
  (48 shorter events, 21.8 us)
Async XLA Ops:
  7.2 338.2 %all-gather.5.cloned.1.call-start = ((), (), s32[]{:S(2)}) async-start(), calls=%async_computation | async-start | bytes 16809984 | tf_op jit(solution)/shard_map/all_gather | solution.py:41
  9.0 23.1 %collective-permute-start.3 = (f32[8,64,64]{1,2,0:T(8,128)S(1)}, f32[8,64,64]{1,2,0:T(8,128)S(1)}, u32[]{:S(2)}, u32[]{:S(2)}) collective-permute-start(f32[8,64,64]{1,2,0:T(8,128)S(1)} %copy_multiply_fusion), channel_id=1, source_target_pairs={{2,0},{3,1},{4,2},{5,3},{6,4},{7,5},{8,6},{9,7},{10,8},{11,9},{12,... | collective-permute-start | bytes 393224 | tf_op jit(solution)/shard_map/ppermute | solution.py:12
  10.3 21.8 %collective-permute-start.2 = (f32[8,64,64]{1,2,0:T(8,128)S(1)}, f32[8,64,64]{1,2,0:T(8,128)S(1)}, u32[]{:S(2)}, u32[]{:S(2)}) collective-permute-start(f32[8,64,64]{1,2,0:T(8,128)S(1)} %copy_multiply_fusion), channel_id=1, source_target_pairs={{1,0},{2,1},{3,2},{4,3},{5,4},{6,5},{7,6},{8,7},{9,8},{10,9},{11,1... | collective-permute-start | bytes 393224 | tf_op jit(solution)/shard_map/ppermute | solution.py:12
  19.1 12.9 %collective-permute-start.1 = (f32[8,64,64]{1,2,0:T(8,128)S(1)}, f32[8,64,64]{1,2,0:T(8,128)S(1)}, u32[]{:S(2)}, u32[]{:S(2)}) collective-permute-start(f32[8,64,64]{1,2,0:T(8,128)S(1)} %copy_multiply_fusion), channel_id=1, source_target_pairs={{0,1},{1,2},{2,3},{3,4},{4,5},{5,6},{6,7},{7,8},{8,9},{9,10},{10,1... | collective-permute-start | bytes 393224 | tf_op jit(solution)/shard_map/ppermute | solution.py:12
  23.2 8.7 %collective-permute-start = (f32[8,64,64]{1,2,0:T(8,128)S(1)}, f32[8,64,64]{1,2,0:T(8,128)S(1)}, u32[]{:S(2)}, u32[]{:S(2)}) collective-permute-start(f32[8,64,64]{1,2,0:T(8,128)S(1)} %copy_multiply_fusion), channel_id=1, source_target_pairs={{0,2},{1,3},{2,4},{3,5},{4,6},{5,7},{6,8},{7,9},{8,10},{9,11},{10,... | collective-permute-start | bytes 393224 | tf_op jit(solution)/shard_map/ppermute | solution.py:12
  64.8 10.2 %collective-permute-start.4 = (f32[8,64,64]{1,2,0:T(8,128)S(1)}, f32[8,64,64]{1,2,0:T(8,128)S(1)}, u32[]{:S(2)}, u32[]{:S(2)}) collective-permute-start(f32[8,64,64]{1,2,0:T(8,128)S(1)} %fusion.4), channel_id=1, source_target_pairs={{0,2},{1,3},{2,4},{3,5},{4,6},{5,7},{6,8},{7,9},{8,10},{9,11},{10,... | collective-permute-start | bytes 393224 | tf_op jit(solution)/shard_map/ppermute | solution.py:12
  69.0 8.9 %collective-permute-start.5 = (f32[8,64,64]{1,2,0:T(8,128)S(1)}, f32[8,64,64]{1,2,0:T(8,128)S(1)}, u32[]{:S(2)}, u32[]{:S(2)}) collective-permute-start(f32[8,64,64]{1,2,0:T(8,128)S(1)} %fusion.4), channel_id=1, source_target_pairs={{0,1},{1,2},{2,3},{3,4},{4,5},{5,6},{6,7},{7,8},{8,9},{9,10},{10,1... | collective-permute-start | bytes 393224 | tf_op jit(solution)/shard_map/ppermute | solution.py:12
  71.7 12.9 %collective-permute-start.7 = (f32[8,64,64]{1,2,0:T(8,128)S(1)}, f32[8,64,64]{1,2,0:T(8,128)S(1)}, u32[]{:S(2)}, u32[]{:S(2)}) collective-permute-start(f32[8,64,64]{1,2,0:T(8,128)S(1)} %fusion.4), channel_id=1, source_target_pairs={{2,0},{3,1},{4,2},{5,3},{6,4},{7,5},{8,6},{9,7},{10,8},{11,9},{12,... | collective-permute-start | bytes 393224 | tf_op jit(solution)/shard_map/ppermute | solution.py:12
  73.1 11.4 %collective-permute-start.6 = (f32[8,64,64]{1,2,0:T(8,128)S(1)}, f32[8,64,64]{1,2,0:T(8,128)S(1)}, u32[]{:S(2)}, u32[]{:S(2)}) collective-permute-start(f32[8,64,64]{1,2,0:T(8,128)S(1)} %fusion.4), channel_id=1, source_target_pairs={{1,0},{2,1},{3,2},{4,3},{5,4},{6,5},{7,6},{8,7},{9,8},{10,9},{11,1... | collective-permute-start | bytes 393224 | tf_op jit(solution)/shard_map/ppermute | solution.py:12
  118.3 462.9 %all-gather.7.cloned.1.call-start = ((), (), s32[]{:S(2)}) async-start(), calls=%async_computation.1 | async-start | bytes 16809984 | tf_op jit(solution)/shard_map/all_gather | solution.py:41
Sparse Core Ops, SparseCore 0:
  118.5 226.8 all-gather.4
  365.8 215.3 all-gather.6
